TPU v7x, 128 devices: a whole 4x4x4 slice. The times are simulated.
128 devices in a mesh: zone: 2 (over core), dom: 64 (over y, z, x).
Axes of the slice: x: 4, y: 4, z: 4, core: 2. Of those that a mesh axis runs over, the one named last changes fastest.
Arguments:
- adjoint_start: float32 [2, 32, 196608], P('zone', None, 'dom'), may hold values from -6 to 6
- right_side: float32 [2, 32, 196608], P('zone', None, 'dom'), may hold values from -6 to 6
- send_rows: int32 [2, 64, 64, 24], P('zone', 'dom'), may hold values from 0 to 3071, as said below
- send_count: int32 [2, 64, 64], P('zone', 'dom'), may hold values from 0 to 24, as said below
- face_left: int32 [98304], P('dom'), may hold values from 0 to 511
- face_right: int32 [98304], P('dom'), may hold values from 0 to 768, as said below
- block_left: bfloat16 [6, 6, 98304], P(None, None, 'dom'), may hold values from -1.75 to 1.75
- block_right: bfloat16 [6, 6, 98304], P(None, None, 'dom'), may hold values from -1.75 to 1.75
- cell_diag: bfloat16 [6, 6, 32768], P(None, None, 'dom'), may hold values from -1.61 to 6.65
- cell_prec: bfloat16 [6, 6, 32768], P(None, None, 'dom'), may hold values from -0.162 to 0.49
- elem_nodes: int32 [27, 24576], P(None, 'dom'), may hold values from 0 to 4607, as said below
- elem_mat: bfloat16 [27, 27, 24576], P(None, None, 'dom'), may hold values from -0.65 to 2
- elem_count: int32 [64], P('dom'), may hold values from 192 to 384, as said below
- node_scale: float32 [196608], P('dom'), may hold values from 0.1 to 0.3
- iface_cell: int32 [16384], P('dom'), may hold values from 0 to 511
- iface_slot: int32 [4, 16384], P(None, 'dom'), may hold values from 0 to 2047, as said below
- iface_weight: float32 [4, 16384], P(None, 'dom'), may hold values from 0.05 to 0.45
- flux_in: float32 [6, 16384], P(None, 'dom'), may hold values from -6 to 6
- flux_out: float32 [6, 16384], P(None, 'dom'), may hold values from -3 to 3
- iface_count: int32 [64], P('dom'), may hold values from 64 to 256, as said below
- iface_nodes: int32 [64, 64, 32], P('dom'), may hold values from 0 to 3071
- iface_pairs: int32 [64, 64], P('dom'), may hold values from 0 to 32, as said below
Outputs:
- adjoint: float32 [2, 32, 196608], P('zone', None, 'dom')
- residual: float32 [2, 32, 196608], P('zone', None, 'dom')
Inputs may be any that keep to these rules, and one draw needn't show every extreme that they name: `send_rows`: slots at or beyond a list's count carry no data. In zone 0 every group of 6 slots 6j to 6j + 5 lists the rows v * 512 + c, v = 0 to 5, of one cell c. `send_count`: counts of zone 0 are multiples of 6; a subdomain sends nothing to itself; some list of each zone is full. `face_right`: below 512 the subdomain's own cells; 512 + p * 4 + j the ghost cell j from subdomain p, always with 6 j below that list's count; 768 the wall. `elem_nodes`: below 3072 the subdomain's own rows; 3072 + p * 24 + g the ghost slot g from subdomain p, always with g below that list's count. `elem_count`: live elements are the first ones of a subdomain; some subdomain has 384. `iface_slot`: p * 32 + k names slot k of solid subdomain p's list for this fluid subdomain, always with k below that list's count. `iface_count`: live faces are the first ones of a subdomain; some subdomain has 256. `iface_pairs`: rows are solid subdomain s, columns fluid subdomain f; the pair s = f has 16 or more; some list is full.
All inputs are finite; a program needn't handle non-finite values.
Results may differ from a plain program's by a relative error of at most 0.0003.
Values sent between devices are 32-bit elements; how exact they have to be, the bound alone decides.
A program may use at most 128 MiB of HBM per device.

v0:
```python
import jax
import jax.numpy as jnp
from jax import lax
from jax.experimental import pallas as pl
from jax.experimental.pallas import tpu as pltpu
from jax.sharding import PartitionSpec as P

MESH = pl.DeviceIdType.MESH
F32 = jnp.float32
BF16 = jnp.bfloat16
I32 = jnp.int32
EXACT = lax.Precision.HIGHEST

SWEEPS = 2
COLS = 32
NV = 6
CELLS = 512
ROWS = 3072
FACES = 1536
ELEMS = 384
NODES = 27
GHOST = 24
SLOTS = 32
IFACES = 256
PEERS = 64
LANES = PEERS * 8
EXTRA = 3 * LANES
ELEM_LANES = 28 * ELEMS
BASE = 256


def iota(shape, dim):
    return lax.broadcasted_iota(I32, shape, dim)


def dot(a, b):
    return jnp.dot(a, b, preferred_element_type=F32)


def dot_t(a, b):
    return lax.dot_general(a, b, (((1,), (1,)), ((), ())), preferred_element_type=F32)


def dot_exact(a, b):
    return jnp.dot(a, b, precision=EXACT, preferred_element_type=F32)


def split(x):
    hi = x.astype(BF16)
    lo = (x - hi.astype(F32)).astype(BF16)
    return hi, lo


def onehot(ids, count):
    return jnp.where(iota((count, ids.shape[1]), 0) == ids, 1.0, 0.0).astype(BF16)


def eight(row):
    return jnp.broadcast_to(row, (8, row.shape[1]))


def to_int(x):
    return (x + 0.5).astype(I32)


def pick_mask():
    return jnp.where(iota((PEERS, LANES), 0) == (iota((PEERS, LANES), 1) >> 3), 1.0, 0.0)


def spread_ids(table, lane_slot, mask):
    width = table.shape[1]
    chooser = jnp.where(iota((width, LANES), 0) == lane_slot, 1.0, 0.0)
    return to_int(jnp.sum(dot_exact(table, chooser) * mask, axis=0, keepdims=True))


def chunked(total, step, body):
    def run(k, carry):
        body(pl.multiple_of(k * step, 128))
        return carry

    lax.fori_loop(0, total // step, run, 0)


def wide_gather(xh, xl, blocks, hot, tags, total, step, put):
    def body(off):
        lanes = pl.ds(off, step)
        onto = hot[:, lanes]
        found = dot(xh[0 : blocks * COLS, :], onto) + dot(xl[0 : blocks * COLS, :], onto)
        tag = tags[:, lanes]
        parts = []
        for g in range(COLS // 8):
            part = jnp.zeros((8, step), F32)
            for a in range(blocks):
                r = a * COLS + g * 8
                part = jnp.where(tag == a, found[r : r + 8, :], part)
            parts.append(part)
        put(off, jnp.concatenate(parts, axis=0))

    chunked(total, step, body)


def wide_scatter(fetch, blocks, hot, tags, total, step, acc):
    acc[0 : blocks * COLS, :] = jnp.zeros((blocks * COLS, BASE), F32)

    def body(off):
        lanes = pl.ds(off, step)
        hi, lo = fetch(off)
        onto = hot[:, lanes]
        tag = tags[:, lanes]
        his, los = [], []
        for a in range(blocks):
            m8 = jnp.where(tag == a, 1.0, 0.0)
            m = jnp.concatenate([m8, m8, m8, m8], axis=0).astype(BF16)
            his.append(hi * m)
            los.append(lo * m)
        sum_hi = dot_t(jnp.concatenate(his, axis=0), onto)
        sum_lo = dot_t(jnp.concatenate(los, axis=0), onto)
        acc[0 : blocks * COLS, :] += sum_hi + sum_lo

    chunked(total, step, body)


def put_blocks(xh, xl, first, blocks):
    for k, block in enumerate(blocks):
        rows = slice((first + k) * COLS, (first + k + 1) * COLS)
        hi, lo = split(block)
        xh[rows, :] = hi
        xl[rows, :] = lo


def to_tiles(stacked):
    height = stacked.shape[0]
    if height < 128:
        stacked = jnp.concatenate([stacked, jnp.zeros((128 - height, LANES), F32)], axis=0)
    return stacked.T.reshape(PEERS, 8, 128)


def from_tiles(tiles):
    return tiles.reshape(LANES, 128).T


def kernel(
    adjoint_start,
    right_side,
    send_rows,
    send_count,
    face_left,
    face_right,
    block_left,
    block_right,
    cell_diag,
    cell_prec,
    elem_nodes,
    elem_mat,
    elem_count,
    node_scale,
    iface_cell,
    iface_slot,
    iface_weight,
    flux_in,
    flux_out,
    iface_count,
    iface_nodes,
    iface_pairs,
    out_x,
    out_r,
    ghost_tx,
    ghost_rx,
    back_tx,
    back_rx,
    pair_tx,
    pair_rx,
    fx,
    f_coupling,
    f_image,
    f_jump,
    f_right,
    f_both,
    f_diff,
    f_left,
    f_send,
    f_cell,
    f_slot,
    f_slot_tag,
    sx,
    s_coupling,
    s_mat,
    s_nodes,
    s_send,
    s_send_tag,
    s_pair,
    s_pair_tag,
    s_elem,
    s_elem_tag,
    s_picked,
    s_hi,
    s_lo,
    s_wide,
    xh,
    xl,
    acc,
    ghost_send_sem,
    ghost_recv_sem,
    back_send_sem,
    back_recv_sem,
    pair_send_sem,
    pair_recv_sem,
):
    zone = lax.axis_index("zone")
    me = lax.axis_index("dom")
    other = 1 - zone
    is_fluid = zone == 0
    is_solid = zone == 1

    barrier = pltpu.get_barrier_semaphore()

    def greet(i, carry):
        peer = lax.rem(me + i, PEERS)
        pl.semaphore_signal(barrier, inc=1, device_id=(zone, peer), device_id_type=MESH)
        return carry

    def greet_other(i, carry):
        peer = lax.rem(me + i, PEERS)
        pl.semaphore_signal(barrier, inc=1, device_id=(other, peer), device_id_type=MESH)
        return carry

    lax.fori_loop(1, PEERS, greet, 0)
    lax.fori_loop(0, PEERS, greet_other, 0)

    def copy_to(src, dst, peer, to_zone, send_sem, recv_sem):
        return pltpu.make_async_remote_copy(
            src_ref=src.at[peer],
            dst_ref=dst.at[me],
            send_sem=send_sem,
            recv_sem=recv_sem,
            device_id=(to_zone, peer),
            device_id_type=MESH,
        )

    def send_all(src, dst, to_zone, first, send_sem, recv_sem):
        def start(i, carry):
            peer = lax.rem(me + i, PEERS)
            copy_to(src, dst, peer, to_zone, send_sem, recv_sem).start()
            return carry

        lax.fori_loop(first, PEERS, start, 0)

    def all_of(src, dst, to_zone, count, send_sem, recv_sem):
        return pltpu.make_async_remote_copy(
            src_ref=src.at[pl.ds(0, count)],
            dst_ref=dst.at[pl.ds(0, count)],
            send_sem=send_sem,
            recv_sem=recv_sem,
            device_id=(to_zone, lax.rem(me + 1, PEERS)),
            device_id_type=MESH,
        )

    counts = send_count[0].astype(F32)
    lane_row = iota((1, LANES), 1)

    def expand(row, mask):
        return to_int(dot_exact(row, mask))

    lane_half = (iota((96, LANES), 1) >> 2) & 1

    def halves(two):
        return jnp.where(lane_half == 0, two[0:96, :], two[96:192, :])

    def widen(one):
        zero = jnp.zeros((96, LANES), F32)
        return jnp.concatenate(
            [jnp.where(lane_half == 0, one, zero), jnp.where(lane_half == 1, one, zero)], axis=0
        )

    def times(values, hot):
        hi, lo = split(values)
        both = dot(jnp.concatenate([hi, lo], axis=0), hot)
        rows = values.shape[0]
        return both[0:rows] + both[rows : 2 * rows]

    def times_t(values, hot):
        hi, lo = split(values)
        both = dot_t(jnp.concatenate([hi, lo], axis=0), hot)
        rows = values.shape[0]
        return both[0:rows] + both[rows : 2 * rows]

    def fluid_ghosts():
        return to_tiles(halves(times(fx[...], f_send[...])))

    def fluid_first():
        for v in range(NV):
            fx[v * COLS : (v + 1) * COLS, :] = adjoint_start[0, :, v * CELLS : (v + 1) * CELLS]
        mask = pick_mask()
        slot = 6 * (lane_row & 3)
        ids = spread_ids(send_rows[0, 0].astype(F32), slot, mask)
        ids = jnp.where(slot < expand(counts, mask), ids, -1)
        f_send[...] = onehot(ids, CELLS)
        ghost_tx[0] = fluid_ghosts()

    def fluid_pair():
        f_cell[...] = onehot(iface_cell[...], CELLS)
        s = iface_slot[...]
        place = ((s >> 3) & 3) * LANES + (s >> 5) * 8 + (s & 7)
        for a in range(4):
            lanes = slice(a * IFACES, (a + 1) * IFACES)
            f_slot[:, lanes] = onehot(place[a : a + 1, :] & (BASE - 1), BASE)
            f_slot_tag[:, lanes] = eight(place[a : a + 1, :] >> 8)
        at = times(fx[...], f_cell[...])
        live = iota((1, IFACES), 1) < iface_count[0]
        heat = flux_out[0:1, :] * at[0:COLS, :]
        for v in range(1, NV):
            heat = heat + flux_out[v : v + 1, :] * at[v * COLS : (v + 1) * COLS, :]
        heat = jnp.where(live, heat, 0.0)
        for a in range(4):
            lanes = slice(a * IFACES, (a + 1) * IFACES)
            hi, lo = split(iface_weight[a : a + 1, :] * heat)
            s_hi[:, lanes] = hi
            s_lo[:, lanes] = lo

        def fetch(off):
            return s_hi[:, pl.ds(off, 1024)], s_lo[:, pl.ds(off, 1024)]

        wide_scatter(fetch, 8, f_slot, f_slot_tag, 1024, 1024, acc)
        rows = [
            jnp.concatenate(
                [acc[2 * q * COLS : (2 * q + 1) * COLS, :], acc[(2 * q + 1) * COLS : (2 * q + 2) * COLS, :]],
                axis=1,
            )
            for q in range(4)
        ]
        pair_tx[...] = to_tiles(jnp.concatenate(rows, axis=0))

    def fluid_prepare():
        left_io = iota((CELLS, 256), 0)
        ghost_io = CELLS + (left_io >> 3) * 4 + (left_io & 3)

        def body(off):
            lanes = pl.ds(off, 256)
            left = jnp.where(left_io == face_left[:, lanes], 1.0, 0.0)
            right = jnp.where(left_io == face_right[:, lanes], 1.0, 0.0)
            ghost = jnp.where(ghost_io == face_right[:, lanes], 1.0, 0.0)
            f_left[:, lanes] = left.astype(BF16)
            f_diff[0:CELLS, lanes] = (left - right).astype(BF16)
            f_diff[CELLS : CELLS + LANES, lanes] = (-ghost).astype(BF16)

        chunked(FACES, 256, body)

    def fluid_faces(off):
        lanes = pl.ds(off, 128)
        left = block_left[:, :, lanes].astype(F32)
        right = block_right[:, :, lanes].astype(F32)
        both = left + right
        jumps = [f_jump[b * COLS : (b + 1) * COLS, lanes] for b in range(NV)]
        for a in range(NV):
            rows = slice(a * COLS, (a + 1) * COLS)
            to_right = right[0, a : a + 1, :] * jumps[0]
            to_both = both[0, a : a + 1, :] * jumps[0]
            for b in range(1, NV):
                to_right = to_right + right[b, a : a + 1, :] * jumps[b]
                to_both = to_both + both[b, a : a + 1, :] * jumps[b]
            f_right[rows, lanes] = to_right
            f_both[rows, lanes] = to_both

    def fluid_out(sweep):
        ghost = widen(from_tiles(ghost_rx[sweep])[0:96, :])
        f_jump[...] = times(fx[...], f_diff[0:CELLS, :]) + times(ghost, f_diff[CELLS:, :])
        chunked(FACES, 128, fluid_faces)
        ghost_image = -times_t(f_right[...], f_diff[CELLS:, :])
        back_tx[sweep] = to_tiles(halves(ghost_image))

    def cell_apply(blocks, values, put):
        for chunk in range(CELLS // 128):
            lanes = slice(chunk * 128, (chunk + 1) * 128)
            taken = blocks[:, :, lanes].astype(F32)
            for a in range(NV):
                total = taken[0, a : a + 1, :] * values[0:COLS, lanes]
                for b in range(1, NV):
                    total = total + taken[b, a : a + 1, :] * values[b * COLS : (b + 1) * COLS, lanes]
                put(slice(a * COLS, (a + 1) * COLS), lanes, total)

    def fluid_own(sweep):
        f_image[...] = times_t(f_both[...], f_left[...]) - times_t(f_right[...], f_diff[0:CELLS, :])

        def put(rows, lanes, total):
            f_image[rows, lanes] += total

        cell_apply(cell_diag, fx, put)

    def fluid_coupling():
        arrived = from_tiles(pair_rx[...])
        blocks = []
        for q in range(4):
            rows = arrived[q * COLS : (q + 1) * COLS, :]
            blocks += [rows[:, 0:BASE], rows[:, BASE:LANES]]
        put_blocks(xh, xl, 0, blocks)

        def put(off, found):
            s_picked[:, pl.ds(off, 1024)] = found

        wide_gather(xh, xl, 8, f_slot, f_slot_tag, 1024, 1024, put)
        live = iota((1, IFACES), 1) < iface_count[0]
        wall = iface_weight[0:1, :] * s_picked[:, 0:IFACES]
        for a in range(1, 4):
            wall = wall + iface_weight[a : a + 1, :] * s_picked[:, a * IFACES : (a + 1) * IFACES]
        wall = jnp.where(live, wall, 0.0)
        added = jnp.concatenate([flux_in[v : v + 1, :] * wall for v in range(NV)], axis=0)
        f_coupling[...] = times_t(added, f_cell[...])

    def fluid_update(sweep):
        returned = widen(from_tiles(back_rx[sweep])[0:96, :])
        f_image[...] += times_t(returned, f_send[...]) + f_coupling[...]
        for v in range(NV):
            rows = slice(v * COLS, (v + 1) * COLS)
            f_image[rows, :] = right_side[0, :, v * CELLS : (v + 1) * CELLS] - f_image[rows, :]

        def put(rows, lanes, total):
            fx[rows, lanes] += total

        cell_apply(cell_prec, f_image, put)

    def fluid_last():
        for v in range(NV):
            rows = slice(v * COLS, (v + 1) * COLS)
            out_x[0, :, v * CELLS : (v + 1) * CELLS] = fx[rows, :]
            out_r[0, :, v * CELLS : (v + 1) * CELLS] = f_image[rows, :]

    def load_own():
        put_blocks(xh, xl, 0, [sx[:, k * BASE : (k + 1) * BASE] for k in range(ROWS // BASE)])

    def list_rows(table, width, counted, hot, tags):
        mask = pick_mask()
        amount = expand(counted, mask)
        values = table.astype(F32)
        for q in range(width // 8):
            slot = q * 8 + (lane_row & 7)
            ids = spread_ids(values, slot, mask)
            lanes = slice(q * LANES, (q + 1) * LANES)
            hot[:, lanes] = onehot(ids & (BASE - 1), BASE)
            tags[:, lanes] = eight(jnp.where(slot < amount, ids >> 8, -1))

    def gather_lists(parts, hot, tags):
        def put(off, found):
            s_wide[:, pl.ds(off, LANES)] = found

        wide_gather(xh, xl, ROWS // BASE, hot, tags, parts * LANES, LANES, put)
        return to_tiles(
            jnp.concatenate([s_wide[:, q * LANES : (q + 1) * LANES] for q in range(parts)], axis=0)
        )

    def scatter_lists(tiles, parts, hot, tags):
        arrived = from_tiles(tiles)
        for q in range(parts):
            lanes = slice(q * LANES, (q + 1) * LANES)
            hi, lo = split(arrived[q * COLS : (q + 1) * COLS, :])
            s_hi[:, lanes] = hi
            s_lo[:, lanes] = lo

        def fetch(off):
            return s_hi[:, pl.ds(off, LANES)], s_lo[:, pl.ds(off, LANES)]

        wide_scatter(fetch, ROWS // BASE, hot, tags, parts * LANES, LANES, acc)

    def solid_first():
        sx[...] = adjoint_start[0]
        load_own()
        list_rows(send_rows[0, 0], GHOST, counts, s_send, s_send_tag)
        ghost_tx[0] = gather_lists(3, s_send, s_send_tag)

    def solid_pair():
        list_rows(iface_nodes[0], SLOTS, iface_pairs[...].astype(F32), s_pair, s_pair_tag)
        pair_tx[...] = gather_lists(4, s_pair, s_pair_tag)

    def solid_prepare():
        live = iota((1, ELEMS), 1) < elem_count[0]

        def one(j, carry):
            ids = s_nodes[j][0:1, :]
            m = ids - ROWS
            p = (m * 2731) >> 16
            g = m - p * GHOST
            ghost = ROWS + (g >> 3) * LANES + p * 8 + (g & 7)
            ids = jnp.where(m >= 0, ghost, ids)
            lanes = pl.ds(pl.multiple_of(j * ELEMS, 128), ELEMS)
            s_elem[:, lanes] = onehot(ids & (BASE - 1), BASE)
            s_elem_tag[:, lanes] = eight(jnp.where(live, ids >> 8, -1))
            mat = elem_mat[j].astype(F32)
            for k in range(NODES // 3):
                s_mat[j, k, 0:3, :] = mat[3 * k : 3 * k + 3, :]
            return carry

        for j in range(NODES):
            s_nodes[j] = eight(elem_nodes[j : j + 1, :])
        lax.fori_loop(0, NODES, one, 0)
        spare = slice(NODES * ELEMS, ELEM_LANES)
        s_elem[:, spare] = jnp.zeros((BASE, ELEMS), BF16)
        s_elem_tag[:, spare] = jnp.full((8, ELEMS), -1, I32)
        s_hi[:, spare] = jnp.zeros((COLS, ELEMS), BF16)
        s_lo[:, spare] = jnp.zeros((COLS, ELEMS), BF16)

    def solid_elements():
        def group(k, carry):
            i0 = k * 3
            for chunk in range(ELEMS // 128):
                lanes = slice(chunk * 128, (chunk + 1) * 128)
                sums = [None, None, None]
                for j in range(NODES):
                    v = s_picked[:, j * ELEMS + chunk * 128 : j * ELEMS + chunk * 128 + 128]
                    for n in range(3):
                        term = s_mat[j, k, n : n + 1, lanes] * v
                        sums[n] = term if j == 0 else sums[n] + term
                for n in range(3):
                    hi, lo = split(sums[n])
                    off = pl.multiple_of((i0 + n) * ELEMS + chunk * 128, 128)
                    s_hi[:, pl.ds(off, 128)] = hi
                    s_lo[:, pl.ds(off, 128)] = lo
            return carry

        lax.fori_loop(0, NODES // 3, group, 0)

    def solid_out(sweep):
        arrived = from_tiles(ghost_rx[sweep])
        blocks = []
        for q in range(3):
            rows = arrived[q * COLS : (q + 1) * COLS, :]
            blocks += [rows[:, 0:BASE], rows[:, BASE:LANES]]
        put_blocks(xh, xl, ROWS // BASE, blocks)

        def put(off, found):
            s_picked[:, pl.ds(off, 768)] = found

        wide_gather(xh, xl, 18, s_elem, s_elem_tag, ELEM_LANES, 768, put)
        solid_elements()

        def fetch(off):
            return s_hi[:, pl.ds(off, 768)], s_lo[:, pl.ds(off, 768)]

        wide_scatter(fetch, 18, s_elem, s_elem_tag, ELEM_LANES, 768, acc)
        rows = [
            jnp.concatenate(
                [
                    acc[(12 + 2 * q) * COLS : (13 + 2 * q) * COLS, :],
                    acc[(13 + 2 * q) * COLS : (14 + 2 * q) * COLS, :],
                ],
                axis=1,
            )
            for q in range(3)
        ]
        back_tx[sweep] = to_tiles(jnp.concatenate(rows, axis=0))

    def solid_own():
        for k in range(ROWS // BASE):
            out_r[0, :, k * BASE : (k + 1) * BASE] = acc[k * COLS : (k + 1) * COLS, :]

    def solid_coupling():
        scatter_lists(pair_rx[...], 4, s_pair, s_pair_tag)
        for k in range(ROWS // BASE):
            s_coupling[:, k * BASE : (k + 1) * BASE] = acc[k * COLS : (k + 1) * COLS, :]

    def solid_update(sweep):
        scatter_lists(back_rx[sweep], 3, s_send, s_send_tag)
        for k in range(ROWS // BASE):
            lanes = slice(k * BASE, (k + 1) * BASE)
            image = out_r[0, :, lanes] + acc[k * COLS : (k + 1) * COLS, :]
            residual = right_side[0, :, lanes] - s_coupling[:, lanes] - image
            out_r[0, :, lanes] = residual
            sx[:, lanes] += node_scale[:, lanes] * residual

    for s in range(SWEEPS):
        ghost_rx[s, me] = jnp.zeros((8, 128), F32)
        back_rx[s, me] = jnp.zeros((8, 128), F32)
    pl.when(is_fluid)(fluid_first)
    pl.when(is_solid)(solid_first)
    pl.semaphore_wait(barrier, 2 * PEERS - 1)
    send_all(ghost_tx.at[0], ghost_rx.at[0], zone, 1, ghost_send_sem.at[0], ghost_recv_sem.at[0])
    pl.when(is_fluid)(fluid_pair)
    pl.when(is_solid)(solid_pair)
    send_all(pair_tx, pair_rx, other, 0, pair_send_sem, pair_recv_sem)
    pl.when(is_fluid)(fluid_prepare)
    pl.when(is_solid)(solid_prepare)

    def sweep_step(s, carry):
        def rest(src, dst, send_sem, recv_sem):
            return all_of(src.at[s], dst.at[s], zone, PEERS - 1, send_sem.at[s], recv_sem.at[s])

        @pl.when(s > 0)
        def _():
            @pl.when(is_fluid)
            def _():
                ghost_tx[s] = fluid_ghosts()

            @pl.when(is_solid)
            def _():
                load_own()
                ghost_tx[s] = gather_lists(3, s_send, s_send_tag)

            send_all(
                ghost_tx.at[s], ghost_rx.at[s], zone, 1, ghost_send_sem.at[s], ghost_recv_sem.at[s]
            )

        rest(ghost_tx, ghost_rx, ghost_send_sem, ghost_recv_sem).wait_recv()
        pl.when(is_fluid)(lambda: fluid_out(s))
        pl.when(is_solid)(lambda: solid_out(s))
        send_all(back_tx.at[s], back_rx.at[s], zone, 1, back_send_sem.at[s], back_recv_sem.at[s])
        pl.when(is_fluid)(lambda: fluid_own(s))
        pl.when(is_solid)(solid_own)

        @pl.when(s == 0)
        def _():
            both = all_of(pair_tx, pair_rx, other, PEERS, pair_send_sem, pair_recv_sem)
            both.wait_recv()
            pl.when(is_fluid)(fluid_coupling)
            pl.when(is_solid)(solid_coupling)
            both.wait_send()

        rest(back_tx, back_rx, back_send_sem, back_recv_sem).wait_recv()
        pl.when(is_fluid)(lambda: fluid_update(s))
        pl.when(is_solid)(lambda: solid_update(s))
        rest(ghost_tx, ghost_rx, ghost_send_sem, ghost_recv_sem).wait_send()
        rest(back_tx, back_rx, back_send_sem, back_recv_sem).wait_send()
        return carry

    lax.fori_loop(0, SWEEPS, sweep_step, 0)

    pl.when(is_fluid)(fluid_last)

    @pl.when(is_solid)
    def _():
        out_x[0] = sx[...]


def on_device(*args):
    flat = (4, 5, 13, 14)
    args = [a.reshape(1, -1) if i in flat else a for i, a in enumerate(args)]
    vmem = pl.BlockSpec(memory_space=pltpu.VMEM)
    smem = pl.BlockSpec(memory_space=pltpu.SMEM)
    specs = [smem if i in (12, 19) else vmem for i in range(len(args))]
    out = jax.ShapeDtypeStruct((1, COLS, ROWS), F32)
    tiles = pltpu.VMEM((SWEEPS, PEERS, 8, 128), F32)
    scratch = [
        tiles,
        tiles,
        tiles,
        tiles,
        pltpu.VMEM((PEERS, 8, 128), F32),
        pltpu.VMEM((PEERS, 8, 128), F32),
        pltpu.VMEM((NV * COLS, CELLS), F32),
        pltpu.VMEM((NV * COLS, CELLS), F32),
        pltpu.VMEM((NV * COLS, CELLS), F32),
        pltpu.VMEM((NV * COLS, FACES), F32),
        pltpu.VMEM((NV * COLS, FACES), F32),
        pltpu.VMEM((NV * COLS, FACES), F32),
        pltpu.VMEM((CELLS + LANES, FACES), BF16),
        pltpu.VMEM((CELLS, FACES), BF16),
        pltpu.VMEM((CELLS, LANES), BF16),
        pltpu.VMEM((CELLS, IFACES), BF16),
        pltpu.VMEM((BASE, 4 * IFACES), BF16),
        pltpu.VMEM((8, 4 * IFACES), I32),
        pltpu.VMEM((COLS, ROWS), F32),
        pltpu.VMEM((COLS, ROWS), F32),
        pltpu.VMEM((NODES, NODES // 3, 8, ELEMS), F32),
        pltpu.VMEM((NODES, 8, ELEMS), I32),
        pltpu.VMEM((BASE, EXTRA), BF16),
        pltpu.VMEM((8, EXTRA), I32),
        pltpu.VMEM((BASE, 4 * LANES), BF16),
        pltpu.VMEM((8, 4 * LANES), I32),
        pltpu.VMEM((BASE, ELEM_LANES), BF16),
        pltpu.VMEM((8, ELEM_LANES), I32),
        pltpu.VMEM((COLS, ELEM_LANES), F32),
        pltpu.VMEM((COLS, ELEM_LANES), BF16),
        pltpu.VMEM((COLS, ELEM_LANES), BF16),
        pltpu.VMEM((COLS, 4 * LANES), F32),
        pltpu.VMEM((18 * COLS, BASE), BF16),
        pltpu.VMEM((18 * COLS, BASE), BF16),
        pltpu.VMEM((18 * COLS, BASE), F32),
        pltpu.SemaphoreType.DMA((SWEEPS,)),
        pltpu.SemaphoreType.DMA((SWEEPS,)),
        pltpu.SemaphoreType.DMA((SWEEPS,)),
        pltpu.SemaphoreType.DMA((SWEEPS,)),
        pltpu.SemaphoreType.DMA,
        pltpu.SemaphoreType.DMA,
    ]
    return pl.pallas_call(
        kernel,
        out_shape=(out, out),
        in_specs=specs,
        out_specs=(vmem, vmem),
        scratch_shapes=scratch,
        compiler_params=pltpu.CompilerParams(
            collective_id=0, has_side_effects=True, vmem_limit_bytes=56 * 1024 * 1024
        ),
    )(*args)


def solution(mesh):
    placed = (
        P("zone", None, "dom"),
        P("zone", None, "dom"),
        P("zone", "dom", None, None),
        P("zone", "dom", None),
        P("dom"),
        P("dom"),
        P(None, None, "dom"),
        P(None, None, "dom"),
        P(None, None, "dom"),
        P(None, None, "dom"),
        P(None, "dom"),
        P(None, None, "dom"),
        P("dom"),
        P("dom"),
        P("dom"),
        P(None, "dom"),
        P(None, "dom"),
        P(None, "dom"),
        P(None, "dom"),
        P("dom"),
        P("dom", None, None),
        P("dom", None),
    )
    return jax.shard_map(
        on_device,
        mesh=mesh,
        in_specs=placed,
        out_specs=(P("zone", None, "dom"), P("zone", None, "dom")),
        check_vma=False,
    )
```

profile of v0, /device:TPU:1, one launch (start us, length us, event | category | flops | bytes accessed | tf_op | source)
XLA Modules:
  0.0 93.6 jit_solution(14757484025451741738)
XLA Ops:
  1.9 0.0 copy-start.3
  1.9 0.0 copy-start.2
  1.9 1.3 %reshape.16.face_left = s32[1,1536]{1,0:T(1,128)} reshape(s32[1536]{0:T(1024)} %param.26) | data formatting | bytes 12288 | tf_op jit(solution)/shard_map/reshape | solution.py:633
  3.3 0.0 copy-done.3
  3.3 0.6 reshape.17.face_right
  3.9 0.0 copy-done.2
  3.9 0.0 copy-start.1
  3.9 0.7 copy.24.send_rows
  4.6 0.0 copy-done.1
  4.6 0.7 copy.25.iface_nodes
  5.3 85.7 %shard_map.221 = (f32[1,32,3072]{2,1,0:T(8,128)}, f32[1,32,3072]{2,1,0:T(8,128)}) custom-call(f32[1,32,3072]{2,1,0:T(8,128)} %adjoint_start.1, f32[1,32,3072]{2,1,0:T(8,128)} %right_side.1, s32[1,1,64,24]{3,2,1,0:T(8,128)} %copy.24.send_rows, s32[1,1,64]{2,1,0:T(1,128)} %send_count.1, s32[1,1536]{1,0:T(1,128)} %reshape.16.face_left, ...), custom_call_target="tpu_custom_call" | custom-call | tf_op jit(solution)/shard_map/pallas_call | solution.py:682
  91.0 0.0 copy-start
  91.0 1.8 %copy.30 = f32[1,32,3072]{2,1,0:T(8,128)} copy(f32[1,32,3072]{2,1,0:T(8,128)} %get-tuple-element.4) | data formatting | bytes 786432
  92.9 0.0 copy-done
  92.9 0.7 copy.31
Async XLA Ops:
  1.9 1.3 %copy-start.3 = (s32[1536]{0:T(1024)S(1)}, s32[1536]{0:T(1024)}, u32[]{:S(2)}) copy-start(s32[1536]{0:T(1024)} %param.27) | copy-start | bytes 18436
  1.9 1.9 %copy-start.2 = (s32[1,1,64,24]{2,3,1,0:T(8,128)S(1)}, s32[1,1,64,24]{2,3,1,0:T(8,128)}, u32[]{:S(2)}) copy-start(s32[1,1,64,24]{2,3,1,0:T(8,128)} %param.24) | copy-start | bytes 18436
  3.9 0.7 copy-start.1
  91.0 1.8 %copy-start = (f32[1,32,3072]{2,1,0:T(8,128)S(1)}, f32[1,32,3072]{2,1,0:T(8,128)}, u32[]{:S(2)}) copy-start(f32[1,32,3072]{2,1,0:T(8,128)} %get-tuple-element.5) | copy-start | bytes 1179652
where the time goes:
time: 93.9 us; the launch traced here: 93.6 us
  Pallas kernels  85.7 us (91%)
  local copies, waits for them, and re-layouts  5.89 us (6%)
  between operations  1.96 us (2%)
    pallas_call x1, Pallas kernels, on_device(): pl.pallas_call(kernel, out_shape=(out, out), in_specs=specs, out_specs=(v...  85.7 us
    unnamed x12, local copies, waits for them, and re-layouts  3.99 us
    reshape x2, local copies, waits for them, and re-layouts, on_device(): args = [a.reshape(1, -1) if i in flat else a for i, a in enumerate(args)]  1.9 us

commit v1 on v0

--- a/solution.py
+++ b/solution.py
@@ -27,6 +27,19 @@
 EXTRA = 3 * LANES
 ELEM_LANES = 28 * ELEMS
 BASE = 256
+OWN = ROWS // BASE
+ALL = OWN + EXTRA // BASE
+STEP = 3584
+
+
+def hops(step):
+    return sum(min(k, 4 - k) for k in step)
+
+
+FAR_FIRST = sorted(
+    ((y, z, x) for y in range(4) for z in range(4) for x in range(4)), key=lambda step: -hops(step)
+)
+PEER_STEPS = FAR_FIRST[:-1]
 
 
 def iota(shape, dim):
@@ -55,6 +68,12 @@
     return jnp.where(iota((count, ids.shape[1]), 0) == ids, 1.0, 0.0).astype(BF16)
 
 
+def onehot_turned(row, count):
+    column = eight(row).astype(F32).T[:, 0:1].astype(I32)
+    length = row.shape[1]
+    return jnp.where(iota((length, count), 1) == column, 1.0, 0.0).astype(BF16)
+
+
 def eight(row):
     return jnp.broadcast_to(row, (8, row.shape[1]))
 
@@ -68,9 +87,12 @@
 
 
 def spread_ids(table, lane_slot, mask):
-    width = table.shape[1]
+    width = table.shape[0]
     chooser = jnp.where(iota((width, LANES), 0) == lane_slot, 1.0, 0.0)
-    return to_int(jnp.sum(dot_exact(table, chooser) * mask, axis=0, keepdims=True))
+    spread = lax.dot_general(
+        table, chooser, (((0,), (0,)), ((), ())), precision=EXACT, preferred_element_type=F32
+    )
+    return to_int(jnp.sum(spread * mask, axis=0, keepdims=True))
 
 
 def chunked(total, step, body):
@@ -81,41 +103,42 @@
     lax.fori_loop(0, total // step, run, 0)
 
 
-def wide_gather(xh, xl, blocks, hot, tags, total, step, put):
+def wide_gather(xh, xl, first, last, hot, tags, total, step, out, add=False):
     def body(off):
         lanes = pl.ds(off, step)
         onto = hot[:, lanes]
-        found = dot(xh[0 : blocks * COLS, :], onto) + dot(xl[0 : blocks * COLS, :], onto)
+        rows = slice(first * COLS, last * COLS)
+        found = dot(xh[rows, :], onto) + dot(xl[rows, :], onto)
         tag = tags[:, lanes]
-        parts = []
         for g in range(COLS // 8):
-            part = jnp.zeros((8, step), F32)
-            for a in range(blocks):
-                r = a * COLS + g * 8
+            span = slice(g * 8, (g + 1) * 8)
+            part = out[span, lanes] if add else jnp.zeros((8, step), F32)
+            for a in range(first, last):
+                r = (a - first) * COLS + g * 8
                 part = jnp.where(tag == a, found[r : r + 8, :], part)
-            parts.append(part)
-        put(off, jnp.concatenate(parts, axis=0))
+            out[span, lanes] = part
 
     chunked(total, step, body)
 
 
-def wide_scatter(fetch, blocks, hot, tags, total, step, acc):
-    acc[0 : blocks * COLS, :] = jnp.zeros((blocks * COLS, BASE), F32)
+def wide_scatter(his_ref, los_ref, first, last, turned, tags, total, step, acc):
+    rows = slice(first * COLS, last * COLS)
+    acc[rows, :] = jnp.zeros(((last - first) * COLS, BASE), F32)
 
     def body(off):
         lanes = pl.ds(off, step)
-        hi, lo = fetch(off)
-        onto = hot[:, lanes]
+        hi, lo = his_ref[:, lanes], los_ref[:, lanes]
+        onto = turned[lanes, :]
         tag = tags[:, lanes]
         his, los = [], []
-        for a in range(blocks):
+        for a in range(first, last):
             m8 = jnp.where(tag == a, 1.0, 0.0)
             m = jnp.concatenate([m8, m8, m8, m8], axis=0).astype(BF16)
             his.append(hi * m)
             los.append(lo * m)
-        sum_hi = dot_t(jnp.concatenate(his, axis=0), onto)
-        sum_lo = dot_t(jnp.concatenate(los, axis=0), onto)
-        acc[0 : blocks * COLS, :] += sum_hi + sum_lo
+        sum_hi = dot(jnp.concatenate(his, axis=0), onto)
+        sum_lo = dot(jnp.concatenate(los, axis=0), onto)
+        acc[rows, :] += sum_hi + sum_lo
 
     chunked(total, step, body)
 
@@ -181,16 +204,20 @@
     f_send,
     f_cell,
     f_slot,
+    f_slot_t,
     f_slot_tag,
     sx,
     s_coupling,
     s_mat,
     s_nodes,
     s_send,
+    s_send_t,
     s_send_tag,
     s_pair,
+    s_pair_t,
     s_pair_tag,
     s_elem,
+    s_elem_t,
     s_elem_tag,
     s_picked,
     s_hi,
@@ -214,18 +241,18 @@
 
     barrier = pltpu.get_barrier_semaphore()
 
-    def greet(i, carry):
-        peer = lax.rem(me + i, PEERS)
-        pl.semaphore_signal(barrier, inc=1, device_id=(zone, peer), device_id_type=MESH)
-        return carry
-
-    def greet_other(i, carry):
-        peer = lax.rem(me + i, PEERS)
+    side = 4
+    my, mz, mx = me // (side * side), (me // side) % side, me % side
+
+    def peer_at(step):
+        dy, dz, dx = step
+        return ((my + dy) % side) * side * side + ((mz + dz) % side) * side + (mx + dx) % side
+
+    for step in FAR_FIRST:
+        peer = peer_at(step)
+        if step != (0, 0, 0):
+            pl.semaphore_signal(barrier, inc=1, device_id=(zone, peer), device_id_type=MESH)
         pl.semaphore_signal(barrier, inc=1, device_id=(other, peer), device_id_type=MESH)
-        return carry
-
-    lax.fori_loop(1, PEERS, greet, 0)
-    lax.fori_loop(0, PEERS, greet_other, 0)
 
     def copy_to(src, dst, peer, to_zone, send_sem, recv_sem):
         return pltpu.make_async_remote_copy(
@@ -237,13 +264,9 @@
             device_id_type=MESH,
         )
 
-    def send_all(src, dst, to_zone, first, send_sem, recv_sem):
-        def start(i, carry):
-            peer = lax.rem(me + i, PEERS)
-            copy_to(src, dst, peer, to_zone, send_sem, recv_sem).start()
-            return carry
-
-        lax.fori_loop(first, PEERS, start, 0)
+    def send_all(src, dst, to_zone, steps, send_sem, recv_sem):
+        for step in steps:
+            copy_to(src, dst, peer_at(step), to_zone, send_sem, recv_sem).start()
 
     def all_of(src, dst, to_zone, count, send_sem, recv_sem):
         return pltpu.make_async_remote_copy(
@@ -304,6 +327,7 @@
         for a in range(4):
             lanes = slice(a * IFACES, (a + 1) * IFACES)
             f_slot[:, lanes] = onehot(place[a : a + 1, :] & (BASE - 1), BASE)
+            f_slot_t[lanes, :] = onehot_turned(place[a : a + 1, :] & (BASE - 1), BASE)
             f_slot_tag[:, lanes] = eight(place[a : a + 1, :] >> 8)
         at = times(fx[...], f_cell[...])
         live = iota((1, IFACES), 1) < iface_count[0]
@@ -317,10 +341,7 @@
             s_hi[:, lanes] = hi
             s_lo[:, lanes] = lo
 
-        def fetch(off):
-            return s_hi[:, pl.ds(off, 1024)], s_lo[:, pl.ds(off, 1024)]
-
-        wide_scatter(fetch, 8, f_slot, f_slot_tag, 1024, 1024, acc)
+        wide_scatter(s_hi, s_lo, 0, 8, f_slot_t, f_slot_tag, 1024, 1024, acc)
         rows = [
             jnp.concatenate(
                 [acc[2 * q * COLS : (2 * q + 1) * COLS, :], acc[(2 * q + 1) * COLS : (2 * q + 2) * COLS, :]],
@@ -331,19 +352,16 @@
         pair_tx[...] = to_tiles(jnp.concatenate(rows, axis=0))
 
     def fluid_prepare():
-        left_io = iota((CELLS, 256), 0)
+        left_io = iota((CELLS, 128), 0)
         ghost_io = CELLS + (left_io >> 3) * 4 + (left_io & 3)
-
-        def body(off):
-            lanes = pl.ds(off, 256)
-            left = jnp.where(left_io == face_left[:, lanes], 1.0, 0.0)
-            right = jnp.where(left_io == face_right[:, lanes], 1.0, 0.0)
-            ghost = jnp.where(ghost_io == face_right[:, lanes], 1.0, 0.0)
+        for k in range(FACES // 128):
+            lanes = slice(k * 128, (k + 1) * 128)
+            left = jnp.where(left_io == face_left[k : k + 1, :], 1.0, 0.0)
+            right = jnp.where(left_io == face_right[k : k + 1, :], 1.0, 0.0)
+            ghost = jnp.where(ghost_io == face_right[k : k + 1, :], 1.0, 0.0)
             f_left[:, lanes] = left.astype(BF16)
             f_diff[0:CELLS, lanes] = (left - right).astype(BF16)
             f_diff[CELLS : CELLS + LANES, lanes] = (-ghost).astype(BF16)
-
-        chunked(FACES, 256, body)
 
     def fluid_faces(off):
         lanes = pl.ds(off, 128)
@@ -361,9 +379,12 @@
             f_right[rows, lanes] = to_right
             f_both[rows, lanes] = to_both
 
+    def fluid_early():
+        f_jump[...] = times(fx[...], f_diff[0:CELLS, :])
+
     def fluid_out(sweep):
         ghost = widen(from_tiles(ghost_rx[sweep])[0:96, :])
-        f_jump[...] = times(fx[...], f_diff[0:CELLS, :]) + times(ghost, f_diff[CELLS:, :])
+        f_jump[...] += times(ghost, f_diff[CELLS:, :])
         chunked(FACES, 128, fluid_faces)
         ghost_image = -times_t(f_right[...], f_diff[CELLS:, :])
         back_tx[sweep] = to_tiles(halves(ghost_image))
@@ -394,10 +415,7 @@
             blocks += [rows[:, 0:BASE], rows[:, BASE:LANES]]
         put_blocks(xh, xl, 0, blocks)
 
-        def put(off, found):
-            s_picked[:, pl.ds(off, 1024)] = found
-
-        wide_gather(xh, xl, 8, f_slot, f_slot_tag, 1024, 1024, put)
+        wide_gather(xh, xl, 0, 8, f_slot, f_slot_tag, 1024, 1024, s_picked)
         live = iota((1, IFACES), 1) < iface_count[0]
         wall = iface_weight[0:1, :] * s_picked[:, 0:IFACES]
         for a in range(1, 4):
@@ -427,7 +445,7 @@
     def load_own():
         put_blocks(xh, xl, 0, [sx[:, k * BASE : (k + 1) * BASE] for k in range(ROWS // BASE)])
 
-    def list_rows(table, width, counted, hot, tags):
+    def list_rows(table, width, counted, hot, turned, tags):
         mask = pick_mask()
         amount = expand(counted, mask)
         values = table.astype(F32)
@@ -436,18 +454,16 @@
             ids = spread_ids(values, slot, mask)
             lanes = slice(q * LANES, (q + 1) * LANES)
             hot[:, lanes] = onehot(ids & (BASE - 1), BASE)
+            turned[lanes, :] = onehot_turned(ids & (BASE - 1), BASE)
             tags[:, lanes] = eight(jnp.where(slot < amount, ids >> 8, -1))
 
     def gather_lists(parts, hot, tags):
-        def put(off, found):
-            s_wide[:, pl.ds(off, LANES)] = found
-
-        wide_gather(xh, xl, ROWS // BASE, hot, tags, parts * LANES, LANES, put)
+        wide_gather(xh, xl, 0, OWN, hot, tags, parts * LANES, parts * LANES, s_wide)
         return to_tiles(
             jnp.concatenate([s_wide[:, q * LANES : (q + 1) * LANES] for q in range(parts)], axis=0)
         )
 
-    def scatter_lists(tiles, parts, hot, tags):
+    def scatter_lists(tiles, parts, turned, tags):
         arrived = from_tiles(tiles)
         for q in range(parts):
             lanes = slice(q * LANES, (q + 1) * LANES)
@@ -455,19 +471,16 @@
             s_hi[:, lanes] = hi
             s_lo[:, lanes] = lo
 
-        def fetch(off):
-            return s_hi[:, pl.ds(off, LANES)], s_lo[:, pl.ds(off, LANES)]
-
-        wide_scatter(fetch, ROWS // BASE, hot, tags, parts * LANES, LANES, acc)
+        wide_scatter(s_hi, s_lo, 0, OWN, turned, tags, parts * LANES, parts * LANES, acc)
 
     def solid_first():
         sx[...] = adjoint_start[0]
         load_own()
-        list_rows(send_rows[0, 0], GHOST, counts, s_send, s_send_tag)
+        list_rows(send_rows[0, 0], GHOST, counts, s_send, s_send_t, s_send_tag)
         ghost_tx[0] = gather_lists(3, s_send, s_send_tag)
 
     def solid_pair():
-        list_rows(iface_nodes[0], SLOTS, iface_pairs[...].astype(F32), s_pair, s_pair_tag)
+        list_rows(iface_nodes[0], SLOTS, iface_pairs[...].astype(F32), s_pair, s_pair_t, s_pair_tag)
         pair_tx[...] = gather_lists(4, s_pair, s_pair_tag)
 
     def solid_prepare():
@@ -482,6 +495,7 @@
             ids = jnp.where(m >= 0, ghost, ids)
             lanes = pl.ds(pl.multiple_of(j * ELEMS, 128), ELEMS)
             s_elem[:, lanes] = onehot(ids & (BASE - 1), BASE)
+            s_elem_t[lanes, :] = onehot_turned(ids & (BASE - 1), BASE)
             s_elem_tag[:, lanes] = eight(jnp.where(live, ids >> 8, -1))
             mat = elem_mat[j].astype(F32)
             for k in range(NODES // 3):
@@ -493,6 +507,7 @@
         lax.fori_loop(0, NODES, one, 0)
         spare = slice(NODES * ELEMS, ELEM_LANES)
         s_elem[:, spare] = jnp.zeros((BASE, ELEMS), BF16)
+        s_elem_t[spare, :] = jnp.zeros((ELEMS, BASE), BF16)
         s_elem_tag[:, spare] = jnp.full((8, ELEMS), -1, I32)
         s_hi[:, spare] = jnp.zeros((COLS, ELEMS), BF16)
         s_lo[:, spare] = jnp.zeros((COLS, ELEMS), BF16)
@@ -517,6 +532,9 @@
 
         lax.fori_loop(0, NODES // 3, group, 0)
 
+    def solid_early():
+        wide_gather(xh, xl, 0, OWN, s_elem, s_elem_tag, ELEM_LANES, STEP, s_picked)
+
     def solid_out(sweep):
         arrived = from_tiles(ghost_rx[sweep])
         blocks = []
@@ -525,16 +543,9 @@
             blocks += [rows[:, 0:BASE], rows[:, BASE:LANES]]
         put_blocks(xh, xl, ROWS // BASE, blocks)
 
-        def put(off, found):
-            s_picked[:, pl.ds(off, 768)] = found
-
-        wide_gather(xh, xl, 18, s_elem, s_elem_tag, ELEM_LANES, 768, put)
+        wide_gather(xh, xl, OWN, ALL, s_elem, s_elem_tag, ELEM_LANES, STEP, s_picked, add=True)
         solid_elements()
-
-        def fetch(off):
-            return s_hi[:, pl.ds(off, 768)], s_lo[:, pl.ds(off, 768)]
-
-        wide_scatter(fetch, 18, s_elem, s_elem_tag, ELEM_LANES, 768, acc)
+        wide_scatter(s_hi, s_lo, OWN, ALL, s_elem_t, s_elem_tag, ELEM_LANES, STEP, acc)
         rows = [
             jnp.concatenate(
                 [
@@ -548,16 +559,17 @@
         back_tx[sweep] = to_tiles(jnp.concatenate(rows, axis=0))
 
     def solid_own():
+        wide_scatter(s_hi, s_lo, 0, OWN, s_elem_t, s_elem_tag, ELEM_LANES, STEP, acc)
         for k in range(ROWS // BASE):
             out_r[0, :, k * BASE : (k + 1) * BASE] = acc[k * COLS : (k + 1) * COLS, :]
 
     def solid_coupling():
-        scatter_lists(pair_rx[...], 4, s_pair, s_pair_tag)
+        scatter_lists(pair_rx[...], 4, s_pair_t, s_pair_tag)
         for k in range(ROWS // BASE):
             s_coupling[:, k * BASE : (k + 1) * BASE] = acc[k * COLS : (k + 1) * COLS, :]
 
     def solid_update(sweep):
-        scatter_lists(back_rx[sweep], 3, s_send, s_send_tag)
+        scatter_lists(back_rx[sweep], 3, s_send_t, s_send_tag)
         for k in range(ROWS // BASE):
             lanes = slice(k * BASE, (k + 1) * BASE)
             image = out_r[0, :, lanes] + acc[k * COLS : (k + 1) * COLS, :]
@@ -570,13 +582,13 @@
         back_rx[s, me] = jnp.zeros((8, 128), F32)
     pl.when(is_fluid)(fluid_first)
     pl.when(is_solid)(solid_first)
-    pl.semaphore_wait(barrier, 2 * PEERS - 1)
-    send_all(ghost_tx.at[0], ghost_rx.at[0], zone, 1, ghost_send_sem.at[0], ghost_recv_sem.at[0])
     pl.when(is_fluid)(fluid_pair)
     pl.when(is_solid)(solid_pair)
-    send_all(pair_tx, pair_rx, other, 0, pair_send_sem, pair_recv_sem)
     pl.when(is_fluid)(fluid_prepare)
     pl.when(is_solid)(solid_prepare)
+    pl.semaphore_wait(barrier, 2 * PEERS - 1)
+    send_all(ghost_tx.at[0], ghost_rx.at[0], zone, PEER_STEPS, ghost_send_sem.at[0], ghost_recv_sem.at[0])
+    send_all(pair_tx, pair_rx, other, FAR_FIRST, pair_send_sem, pair_recv_sem)
 
     def sweep_step(s, carry):
         def rest(src, dst, send_sem, recv_sem):
@@ -594,13 +606,15 @@
                 ghost_tx[s] = gather_lists(3, s_send, s_send_tag)
 
             send_all(
-                ghost_tx.at[s], ghost_rx.at[s], zone, 1, ghost_send_sem.at[s], ghost_recv_sem.at[s]
+                ghost_tx.at[s], ghost_rx.at[s], zone, PEER_STEPS, ghost_send_sem.at[s], ghost_recv_sem.at[s]
             )
 
+        pl.when(is_fluid)(fluid_early)
+        pl.when(is_solid)(solid_early)
         rest(ghost_tx, ghost_rx, ghost_send_sem, ghost_recv_sem).wait_recv()
         pl.when(is_fluid)(lambda: fluid_out(s))
         pl.when(is_solid)(lambda: solid_out(s))
-        send_all(back_tx.at[s], back_rx.at[s], zone, 1, back_send_sem.at[s], back_recv_sem.at[s])
+        send_all(back_tx.at[s], back_rx.at[s], zone, PEER_STEPS, back_send_sem.at[s], back_recv_sem.at[s])
         pl.when(is_fluid)(lambda: fluid_own(s))
         pl.when(is_solid)(solid_own)
 
@@ -629,8 +643,13 @@
 
 
 def on_device(*args):
-    flat = (4, 5, 13, 14)
-    args = [a.reshape(1, -1) if i in flat else a for i, a in enumerate(args)]
+    args = list(args)
+    args[2] = args[2].transpose(0, 1, 3, 2)
+    args[4] = args[4].reshape(-1, 128)
+    args[5] = args[5].reshape(-1, 128)
+    args[13] = args[13].reshape(1, -1)
+    args[14] = args[14].reshape(1, -1)
+    args[20] = args[20].transpose(0, 2, 1)
     vmem = pl.BlockSpec(memory_space=pltpu.VMEM)
     smem = pl.BlockSpec(memory_space=pltpu.SMEM)
     specs = [smem if i in (12, 19) else vmem for i in range(len(args))]
@@ -654,16 +673,20 @@
         pltpu.VMEM((CELLS, LANES), BF16),
         pltpu.VMEM((CELLS, IFACES), BF16),
         pltpu.VMEM((BASE, 4 * IFACES), BF16),
+        pltpu.VMEM((4 * IFACES, BASE), BF16),
         pltpu.VMEM((8, 4 * IFACES), I32),
         pltpu.VMEM((COLS, ROWS), F32),
         pltpu.VMEM((COLS, ROWS), F32),
         pltpu.VMEM((NODES, NODES // 3, 8, ELEMS), F32),
         pltpu.VMEM((NODES, 8, ELEMS), I32),
         pltpu.VMEM((BASE, EXTRA), BF16),
+        pltpu.VMEM((EXTRA, BASE), BF16),
         pltpu.VMEM((8, EXTRA), I32),
         pltpu.VMEM((BASE, 4 * LANES), BF16),
+        pltpu.VMEM((4 * LANES, BASE), BF16),
         pltpu.VMEM((8, 4 * LANES), I32),
         pltpu.VMEM((BASE, ELEM_LANES), BF16),
+        pltpu.VMEM((ELEM_LANES, BASE), BF16),
         pltpu.VMEM((8, ELEM_LANES), I32),
         pltpu.VMEM((COLS, ELEM_LANES), F32),
         pltpu.VMEM((COLS, ELEM_LANES), BF16),

time: 93.9 us -> 68.6 us (0.73)
  Pallas kernels: 85.7 us -> 63.9 us
  local copies, waits for them, and re-layouts: 5.89 us -> 2.57 us
    pallas_call x1, Pallas kernels: 85.7 us -> 63.9 us  [on_device(): pl.pallas_call(kernel, out_shape=(out, out), in_specs=specs, out_specs=(v...]
    reshape x2 -> x0, local copies, waits for them, and re-layouts: 1.9 us -> none  [on_device(): args = [a.reshape(1, -1) if i in flat else a for i, a in enumerate(args)]]
    unnamed x12 -> x4, local copies, waits for them, and re-layouts: 3.99 us -> 2.57 us
where the time goes in v1:
time: 68.6 us; the launch traced here: 68.4 us
  Pallas kernels  63.9 us (93%)
  local copies, waits for them, and re-layouts  2.57 us (4%)
  between operations  1.95 us (3%)
    pallas_call x1, Pallas kernels, on_device(): pl.pallas_call(kernel, out_shape=(out, out), in_specs=specs, out_specs=(v...  63.9 us
    unnamed x4, local copies, waits for them, and re-layouts  2.57 us

profile of v1, /device:TPU:1, one launch (start us, length us, event | category | flops | bytes accessed | tf_op | source)
XLA Modules:
  0.0 68.4 jit_solution(4049140661044876154)
XLA Ops:
  1.9 63.9 %shard_map.221 = (f32[1,32,3072]{2,1,0:T(8,128)}, f32[1,32,3072]{2,1,0:T(8,128)}) custom-call(f32[1,32,3072]{2,1,0:T(8,128)} %adjoint_start.1, f32[1,32,3072]{2,1,0:T(8,128)} %right_side.1, s32[1,1,24,64]{3,2,1,0:T(8,128)} %bitcast.7, s32[1,1,64]{2,1,0:T(1,128)} %send_count.1, s32[12,128]{1,0:T(8,128)} %bitcast.9, s32[12,128]{1,0:T(8,128)} %bitcast.10, ...), custom_call_target="tpu_custom_call" | custom-call | tf_op jit(solution)/shard_map/pallas_call | solution.py:705
  65.8 0.0 copy-start
  65.8 1.8 %copy.28 = f32[1,32,3072]{2,1,0:T(8,128)} copy(f32[1,32,3072]{2,1,0:T(8,128)} %get-tuple-element.4) | data formatting | bytes 786432
  67.6 0.0 copy-done
  67.6 0.7 %copy.29 = f32[1,32,3072]{2,1,0:T(8,128)} copy(f32[1,32,3072]{2,1,0:T(8,128)S(1)} %copy-done) | data formatting | bytes 786432
Async XLA Ops:
  65.8 1.8 %copy-start = (f32[1,32,3072]{2,1,0:T(8,128)S(1)}, f32[1,32,3072]{2,1,0:T(8,128)}, u32[]{:S(2)}) copy-start(f32[1,32,3072]{2,1,0:T(8,128)} %get-tuple-element.5) | copy-start | bytes 1179652

commit v2 on v1

--- a/solution.py
+++ b/solution.py
@@ -30,6 +30,7 @@
 OWN = ROWS // BASE
 ALL = OWN + EXTRA // BASE
 STEP = 3584
+GROUP = 9
 
 
 def hops(step):
@@ -485,26 +486,32 @@
 
     def solid_prepare():
         live = iota((1, ELEMS), 1) < elem_count[0]
+        ids = elem_nodes[...]
+        m = ids - ROWS
+        p = (m * 2731) >> 16
+        g = m - p * GHOST
+        ids = jnp.where(m >= 0, ROWS + (g >> 3) * LANES + p * 8 + (g & 7), ids)
+        low = ids & (BASE - 1)
+        high = jnp.where(live, ids >> 8, -1)
+        for j in range(NODES):
+            s_nodes[j] = eight(low[j : j + 1, :])
+            s_elem_tag[:, j * ELEMS : (j + 1) * ELEMS] = eight(high[j : j + 1, :])
 
         def one(j, carry):
-            ids = s_nodes[j][0:1, :]
-            m = ids - ROWS
-            p = (m * 2731) >> 16
-            g = m - p * GHOST
-            ghost = ROWS + (g >> 3) * LANES + p * 8 + (g & 7)
-            ids = jnp.where(m >= 0, ghost, ids)
             lanes = pl.ds(pl.multiple_of(j * ELEMS, 128), ELEMS)
-            s_elem[:, lanes] = onehot(ids & (BASE - 1), BASE)
-            s_elem_t[lanes, :] = onehot_turned(ids & (BASE - 1), BASE)
-            s_elem_tag[:, lanes] = eight(jnp.where(live, ids >> 8, -1))
+            s_elem[:, lanes] = onehot(s_nodes[j][0:1, :], BASE)
             mat = elem_mat[j].astype(F32)
-            for k in range(NODES // 3):
-                s_mat[j, k, 0:3, :] = mat[3 * k : 3 * k + 3, :]
+            for k in range(NODES // GROUP):
+                s_mat[j, k, 0:GROUP, :] = mat[GROUP * k : GROUP * k + GROUP, :]
             return carry
 
+        lax.fori_loop(0, NODES, one, 0, unroll=3)
+        padded = jnp.concatenate([low.astype(F32), jnp.zeros((5, ELEMS), F32)], axis=0)
+        columns = padded.T.astype(I32)
         for j in range(NODES):
-            s_nodes[j] = eight(elem_nodes[j : j + 1, :])
-        lax.fori_loop(0, NODES, one, 0)
+            s_elem_t[j * ELEMS : (j + 1) * ELEMS, :] = jnp.where(
+                iota((ELEMS, BASE), 1) == columns[:, j : j + 1], 1.0, 0.0
+            ).astype(BF16)
         spare = slice(NODES * ELEMS, ELEM_LANES)
         s_elem[:, spare] = jnp.zeros((BASE, ELEMS), BF16)
         s_elem_t[spare, :] = jnp.zeros((ELEMS, BASE), BF16)
@@ -514,23 +521,23 @@
 
     def solid_elements():
         def group(k, carry):
-            i0 = k * 3
+            i0 = k * GROUP
             for chunk in range(ELEMS // 128):
                 lanes = slice(chunk * 128, (chunk + 1) * 128)
-                sums = [None, None, None]
+                sums = [None] * GROUP
                 for j in range(NODES):
                     v = s_picked[:, j * ELEMS + chunk * 128 : j * ELEMS + chunk * 128 + 128]
-                    for n in range(3):
+                    for n in range(GROUP):
                         term = s_mat[j, k, n : n + 1, lanes] * v
                         sums[n] = term if j == 0 else sums[n] + term
-                for n in range(3):
+                for n in range(GROUP):
                     hi, lo = split(sums[n])
                     off = pl.multiple_of((i0 + n) * ELEMS + chunk * 128, 128)
                     s_hi[:, pl.ds(off, 128)] = hi
                     s_lo[:, pl.ds(off, 128)] = lo
             return carry
 
-        lax.fori_loop(0, NODES // 3, group, 0)
+        lax.fori_loop(0, NODES // GROUP, group, 0)
 
     def solid_early():
         wide_gather(xh, xl, 0, OWN, s_elem, s_elem_tag, ELEM_LANES, STEP, s_picked)
@@ -677,7 +684,7 @@
         pltpu.VMEM((8, 4 * IFACES), I32),
         pltpu.VMEM((COLS, ROWS), F32),
         pltpu.VMEM((COLS, ROWS), F32),
-        pltpu.VMEM((NODES, NODES // 3, 8, ELEMS), F32),
+        pltpu.VMEM((NODES, NODES // GROUP, 16, ELEMS), F32),
         pltpu.VMEM((NODES, 8, ELEMS), I32),
         pltpu.VMEM((BASE, EXTRA), BF16),
         pltpu.VMEM((EXTRA, BASE), BF16),
@@ -704,7 +711,7 @@
     ]
     return pl.pallas_call(
         kernel,
-        out_shape=(out, out),
+        out_shape=(pltpu.VMEM((1, COLS, ROWS), F32), pltpu.VMEM((1, COLS, ROWS), F32)),
         in_specs=specs,
         out_specs=(vmem, vmem),
         scratch_shapes=scratch,

time: 68.6 us -> 61 us (0.89)
  Pallas kernels: 63.9 us -> 57.4 us
  local copies, waits for them, and re-layouts: 2.57 us -> 1.49 us
    pallas_call x1, Pallas kernels: 63.9 us -> 57.4 us  [on_device(): pl.pallas_call(kernel, out_shape=(pltpu.VMEM((1, COLS, ROWS), F32), pltpu...]
    unnamed x4 -> x2, local copies, waits for them, and re-layouts: 2.57 us -> 1.49 us
where the time goes in v2:
time: 61 us; the launch traced here: 60.8 us
  Pallas kernels  57.4 us (94%)
  between operations  1.94 us (3%)
  local copies, waits for them, and re-layouts  1.49 us (2%)
    pallas_call x1, Pallas kernels, on_device(): pl.pallas_call(kernel, out_shape=(pltpu.VMEM((1, COLS, ROWS), F32), pltpu...  57.4 us
    unnamed x2, local copies, waits for them, and re-layouts  1.49 us

profile of v2, /device:TPU:1, one launch (start us, length us, event | category | flops | bytes accessed | tf_op | source)
XLA Modules:
  0.0 60.8 jit_solution(1550835739828680351)
XLA Ops:
  1.9 57.4 %shard_map.221 = (f32[1,32,3072]{2,1,0:T(8,128)S(1)}, f32[1,32,3072]{2,1,0:T(8,128)S(1)}) custom-call(f32[1,32,3072]{2,1,0:T(8,128)} %adjoint_start.1, f32[1,32,3072]{2,1,0:T(8,128)} %right_side.1, s32[1,1,24,64]{3,2,1,0:T(8,128)} %bitcast.7, s32[1,1,64]{2,1,0:T(1,128)} %send_count.1, s32[12,128]{1,0:T(8,128)} %bitcast.9, s32[12,128]{1,0:T(8,128)} %bitcast.10, ...), custom_call_target="tpu_custom_call" | custom-call | tf_op jit(solution)/shard_map/pallas_call | solution.py:712
  59.3 0.7 %copy.26 = f32[1,32,3072]{2,1,0:T(8,128)} copy(f32[1,32,3072]{2,1,0:T(8,128)S(1)} %get-tuple-element.2) | data formatting | bytes 786432
  60.1 0.7 %copy.27 = f32[1,32,3072]{2,1,0:T(8,128)} copy(f32[1,32,3072]{2,1,0:T(8,128)S(1)} %get-tuple-element.3) | data formatting | bytes 786432

commit v3 on v2

--- a/solution.py
+++ b/solution.py
@@ -550,9 +550,9 @@
             blocks += [rows[:, 0:BASE], rows[:, BASE:LANES]]
         put_blocks(xh, xl, ROWS // BASE, blocks)
 
-        wide_gather(xh, xl, OWN, ALL, s_elem, s_elem_tag, ELEM_LANES, STEP, s_picked, add=True)
+        wide_gather(xh, xl, OWN, ALL, s_elem, s_elem_tag, ELEM_LANES, ELEM_LANES // 2, s_picked, add=True)
         solid_elements()
-        wide_scatter(s_hi, s_lo, OWN, ALL, s_elem_t, s_elem_tag, ELEM_LANES, STEP, acc)
+        wide_scatter(s_hi, s_lo, OWN, ALL, s_elem_t, s_elem_tag, ELEM_LANES, ELEM_LANES, acc)
         rows = [
             jnp.concatenate(
                 [

time: 61 us -> 59.8 us (0.980)
  Pallas kernels: 57.4 us -> 56.2 us
    pallas_call x1, Pallas kernels: 57.4 us -> 56.2 us  [on_device(): pl.pallas_call(kernel, out_shape=(pltpu.VMEM((1, COLS, ROWS), F32), pltpu...]
where the time goes in v3:
time: 59.8 us; the launch traced here: 59.6 us
  Pallas kernels  56.2 us (94%)
  between operations  1.94 us (3%)
  local copies, waits for them, and re-layouts  1.49 us (2%)
    pallas_call x1, Pallas kernels, on_device(): pl.pallas_call(kernel, out_shape=(pltpu.VMEM((1, COLS, ROWS), F32), pltpu...  56.2 us
    unnamed x2, local copies, waits for them, and re-layouts  1.49 us

profile of v3, /device:TPU:1, one launch (start us, length us, event | category | flops | bytes accessed | tf_op | source)
XLA Modules:
  0.0 59.6 jit_solution(7085650484399882022)
XLA Ops:
  1.9 56.2 %shard_map.221 = (f32[1,32,3072]{2,1,0:T(8,128)S(1)}, f32[1,32,3072]{2,1,0:T(8,128)S(1)}) custom-call(f32[1,32,3072]{2,1,0:T(8,128)} %adjoint_start.1, f32[1,32,3072]{2,1,0:T(8,128)} %right_side.1, s32[1,1,24,64]{3,2,1,0:T(8,128)} %bitcast.7, s32[1,1,64]{2,1,0:T(1,128)} %send_count.1, s32[12,128]{1,0:T(8,128)} %bitcast.9, s32[12,128]{1,0:T(8,128)} %bitcast.10, ...), custom_call_target="tpu_custom_call" | custom-call | tf_op jit(solution)/shard_map/pallas_call | solution.py:712
  58.1 0.7 %copy.26 = f32[1,32,3072]{2,1,0:T(8,128)} copy(f32[1,32,3072]{2,1,0:T(8,128)S(1)} %get-tuple-element.2) | data formatting | bytes 786432
  58.9 0.7 %copy.27 = f32[1,32,3072]{2,1,0:T(8,128)} copy(f32[1,32,3072]{2,1,0:T(8,128)S(1)} %get-tuple-element.3) | data formatting | bytes 786432

commit v4 on v3

--- a/solution.py
+++ b/solution.py
@@ -505,7 +505,7 @@
                 s_mat[j, k, 0:GROUP, :] = mat[GROUP * k : GROUP * k + GROUP, :]
             return carry
 
-        lax.fori_loop(0, NODES, one, 0, unroll=3)
+        lax.fori_loop(0, NODES, one, 0, unroll=9)
         padded = jnp.concatenate([low.astype(F32), jnp.zeros((5, ELEMS), F32)], axis=0)
         columns = padded.T.astype(I32)
         for j in range(NODES):
@@ -589,12 +589,12 @@
         back_rx[s, me] = jnp.zeros((8, 128), F32)
     pl.when(is_fluid)(fluid_first)
     pl.when(is_solid)(solid_first)
-    pl.when(is_fluid)(fluid_pair)
-    pl.when(is_solid)(solid_pair)
     pl.when(is_fluid)(fluid_prepare)
     pl.when(is_solid)(solid_prepare)
     pl.semaphore_wait(barrier, 2 * PEERS - 1)
     send_all(ghost_tx.at[0], ghost_rx.at[0], zone, PEER_STEPS, ghost_send_sem.at[0], ghost_recv_sem.at[0])
+    pl.when(is_fluid)(fluid_pair)
+    pl.when(is_solid)(solid_pair)
     send_all(pair_tx, pair_rx, other, FAR_FIRST, pair_send_sem, pair_recv_sem)
 
     def sweep_step(s, carry):

time: 59.8 us -> 59.6 us (level)
  no operation moved by 1% of the time
where the time goes in v4:
time: 59.6 us; the launch traced here: 59.4 us
  Pallas kernels  56 us (94%)
  between operations  1.94 us (3%)
  local copies, waits for them, and re-layouts  1.49 us (2%)
    pallas_call x1, Pallas kernels, on_device(): pl.pallas_call(kernel, out_shape=(pltpu.VMEM((1, COLS, ROWS), F32), pltpu...  56 us
    unnamed x2, local copies, waits for them, and re-layouts  1.49 us

profile of v4, /device:TPU:1, one launch (start us, length us, event | category | flops | bytes accessed | tf_op | source)
XLA Modules:
  0.0 59.4 jit_solution(11946820377543081779)
XLA Ops:
  1.9 56.0 %shard_map.221 = (f32[1,32,3072]{2,1,0:T(8,128)S(1)}, f32[1,32,3072]{2,1,0:T(8,128)S(1)}) custom-call(f32[1,32,3072]{2,1,0:T(8,128)} %adjoint_start.1, f32[1,32,3072]{2,1,0:T(8,128)} %right_side.1, s32[1,1,24,64]{3,2,1,0:T(8,128)} %bitcast.7, s32[1,1,64]{2,1,0:T(1,128)} %send_count.1, s32[12,128]{1,0:T(8,128)} %bitcast.9, s32[12,128]{1,0:T(8,128)} %bitcast.10, ...), custom_call_target="tpu_custom_call" | custom-call | tf_op jit(solution)/shard_map/pallas_call | solution.py:712
  57.9 0.7 %copy.26 = f32[1,32,3072]{2,1,0:T(8,128)} copy(f32[1,32,3072]{2,1,0:T(8,128)S(1)} %get-tuple-element.2) | data formatting | bytes 786432
  58.7 0.7 %copy.27 = f32[1,32,3072]{2,1,0:T(8,128)} copy(f32[1,32,3072]{2,1,0:T(8,128)S(1)} %get-tuple-element.3) | data formatting | bytes 786432
